TPU v7x, 32 devices: a whole 2x2x4 slice. The times are simulated.
32 devices in a mesh: gx: 4 (over y, core), gy: 2 (over x), gz: 4 (over z).
Axes of the slice: x: 2, y: 2, z: 4, core: 2. Of those that a mesh axis runs over, the one named last changes fastest.
Arguments:
- stem: bfloat16 [2, 4, 2, 4, 256, 1024], P(None, 'gx', 'gy', 'gz'), may hold values from -6 to 6
- branch_one: bfloat16 [2, 2, 1024, 1024], replicated, may hold values from -0.125 to 0.125
- branch_two: bfloat16 [2, 2, 1024, 1024], P(None, None, ('gy', 'gz')), may hold values from -0.1875 to 0.1875
- branch_three: bfloat16 [2, 2, 1024, 1024], P(None, None, 'gz'), may hold values from -0.125 to 0.125
- slice_values: int32 [3], replicated, may hold values from 0 to 1, as said below
Outputs:
- contracted: bfloat16 [2, 4, 2, 4, 256, 1024], P(None, 'gx', 'gy', 'gz')
Inputs may be any that keep to these rules, and one draw needn't show every extreme that they name: `slice_values`: the first two slices differ.
All inputs are finite; a program needn't handle non-finite values.
Results may differ from a plain program's by a relative error of at most 0.0057.
Values may be sent and summed in bfloat16 or wider, within the bound.
A program may use at most 128 MiB of HBM per device.

v0:
```python
import jax
import jax.numpy as jnp
from jax import lax
from jax.sharding import PartitionSpec as P

WIDTH = 1024
ROWS = 256


def complex_matrix(branch):
    top_half = jnp.concatenate([branch[0], branch[1]], axis=1)
    bottom_half = jnp.concatenate([-branch[1], branch[0]], axis=1)
    return jnp.concatenate([top_half, bottom_half], axis=0)


def complex_product(operand, branch):
    joined = jnp.concatenate([operand[0], operand[1]], axis=1)
    result = jnp.dot(joined, complex_matrix(branch), preferred_element_type=jnp.float32)
    columns = branch.shape[2]
    return jnp.stack([result[:, :columns], result[:, columns:]])


def split_result(result):
    columns = result.shape[1] // 2
    return jnp.stack([result[:, :columns], result[:, columns:]])


def make_accumulate(operand, shard_rows):
    real_part = operand[0]
    imag_part = operand[1]
    joined = jnp.concatenate([real_part, imag_part], axis=1)
    return jnp.dot(joined, complex_matrix(shard_rows), preferred_element_type=jnp.float32)


def third_contraction(operand, branch_three, slice_values):
    local_third = lax.dynamic_index_in_dim(branch_three, slice_values[2], 0, keepdims=False)
    summed = make_accumulate(operand, lax.all_gather(local_third, "gz", axis=1, tiled=True))
    return split_result(summed).astype(jnp.bfloat16)


def body(stem, branch_one, branch_two, branch_three, slice_values):
    count_gx = lax.axis_size("gx")
    count_gy = lax.axis_size("gy")
    count_gz = lax.axis_size("gz")
    group_one = count_gx * count_gy
    group_two = count_gy * count_gz
    rows_one = ROWS // group_one
    rows_two = ROWS // group_two
    part_one = WIDTH // group_one
    part_two = WIDTH // group_two
    first_branch = lax.dynamic_index_in_dim(branch_one, slice_values[0], 0, keepdims=False)
    arrived = lax.all_to_all(
        stem.reshape(2, 1, group_one, rows_one, WIDTH),
        ("gx", "gy"),
        split_axis=2,
        concat_axis=1,
        tiled=True,
    )
    ordered = arrived.reshape(2, group_one, rows_one, part_one, group_one).transpose(0, 2, 4, 1, 3)
    ordered = ordered.reshape(2, ROWS, WIDTH)
    middle = complex_product(ordered, first_branch).astype(jnp.bfloat16)
    gathered = lax.all_to_all(
        middle.reshape(2, group_two, 1, rows_two, WIDTH),
        ("gy", "gz"),
        split_axis=1,
        concat_axis=2,
        tiled=True,
    )
    regrouped = gathered.reshape(2, group_two, rows_two, part_two, group_two).transpose(
        0, 2, 4, 1, 3
    )
    regrouped = regrouped.reshape(2, ROWS, WIDTH)
    local_second = lax.dynamic_index_in_dim(branch_two, slice_values[1], 0, keepdims=False)
    summed = make_accumulate(
        regrouped, lax.all_gather(local_second, ("gy", "gz"), axis=1, tiled=True)
    )
    second = split_result(summed).astype(jnp.bfloat16)
    returned = lax.all_to_all(
        second.reshape(2, 1, rows_two, group_two, group_two, part_two),
        ("gy", "gz"),
        split_axis=4,
        concat_axis=1,
        tiled=True,
    )
    result = third_contraction(returned.reshape(2, ROWS, WIDTH), branch_three, slice_values)
    return result.reshape(stem.shape)


def solution(mesh):
    return jax.shard_map(
        body,
        mesh=mesh,
        in_specs=(
            P(None, "gx", "gy", "gz", None, None),
            P(),
            P(None, None, ("gy", "gz"), None),
            P(None, None, "gz", None),
            P(),
        ),
        out_specs=P(None, "gx", "gy", "gz", None, None),
        check_vma=False,
    )
```

profile of v0, /device:TPU:0, one launch (start us, length us, event | category | flops | bytes accessed | tf_op | source)
XLA Modules:
  0.0 250.3 jit_solution(15021778729917147188)
XLA Ops:
  6.5 1.4 fusion.52
  9.9 1.9 constant_dynamic-slice_fusion.1
  11.8 1.1 copy.38
  13.0 5.2 %all-to-all-start = ((bf16[2,1,8,32,1024]{4,3,1,0,2:T(8,128)(2,1)}), bf16[2,1,8,32,1024]{4,3,1,0,2:T(8,128)(2,1)S(1)}, u32[]{:S(2)}, u32[]{:S(2)}) async-start(bf16[2,1,8,32,1024]{4,3,1,0,2:T(8,128)(2,1)} %copy.38), calls=%async_computation | async-start | bytes 2097152 | tf_op jit(solution)/shard_map/all_to_all | solution.py:52
  20.1 1.0 constant_dynamic-slice_fusion
  23.1 3.2 %dynamic-slice_bitcast_fusion.1 = bf16[1024,1024]{1,0:T(8,128)(2,1)} fusion(bf16[2,2,1024,1024]{3,2,1,0:T(8,128)(2,1)} %param.6, s32[]{:T(128)S(6)} %select_n.12), kind=kLoop, calls=%fused_computation.32 | loop fusion | bytes 4194308 | tf_op jit(solution)/shard_map/squeeze | solution.py:11
  26.3 3.8 %fusion.47 = (bf16[1024,1024]{1,0:T(8,128)(2,1)}, bf16[1024,1024]{1,0:T(8,128)(2,1)}) fusion(bf16[2,2,1024,1024]{3,2,1,0:T(8,128)(2,1)} %param.6, s32[]{:T(128)S(6)} %select_n.12, s32[]{:T(128)S(6)} %add.15), kind=kLoop, calls=%fused_computation.62 | loop fusion | flops 1048576 | bytes 6291464 | tf_op jit(solution)/shard_map/neg | solution.py:12
  30.1 8.6 %all-to-all-done = bf16[2,1,8,32,1024]{4,3,1,0,2:T(8,128)(2,1)S(1)} async-done(((bf16[2,1,8,32,1024]{4,3,1,0,2:T(8,128)(2,1)}), bf16[2,1,8,32,1024]{4,3,1,0,2:T(8,128)(2,1)S(1)}, u32[]{:S(2)}, u32[]{:S(2)}) %all-to-all-start) | async-done | bytes 1048608 | tf_op jit(solution)/shard_map/all_to_all | solution.py:52
  38.7 3.2 %copy.39 = bf16[2,1,8,32,1024]{3,4,2,0,1:T(8,128)(2,1)} copy(bf16[2,1,8,32,1024]{4,3,1,0,2:T(8,128)(2,1)S(1)} %all-to-all-done) | data formatting | bytes 2097152 | tf_op jit(solution)/shard_map/all_to_all | solution.py:52
  41.8 4.0 %fusion.49 = (bf16[1,32,8,8,128]{1,2,4,3,0:T(8,128)(2,1)}, bf16[1,32,8,8,128]{1,2,4,3,0:T(8,128)(2,1)S(1)}) fusion(bf16[2,32,8,8,128]{1,2,4,3,0:T(8,128)(2,1)} %bitcast.74), kind=kLoop, calls=%fused_computation.64 | loop fusion | bytes 2097152 | tf_op jit(solution)/shard_map/slice | solution.py:17
  45.8 3.5 %copy.40 = bf16[1,32,8,8,128]{4,3,2,1,0:T(8,128)(2,1)S(1)} copy(bf16[1,32,8,8,128]{1,2,4,3,0:T(8,128)(2,1)} %get-tuple-element.9) | data formatting | bytes 1048576 | tf_op jit(solution)/shard_map/slice | solution.py:17
  49.3 2.0 copy.41
  51.5 1.6 copy-done.4
  53.1 4.6 %fusion.30 = bf16[256,2048]{1,0:T(8,128)(2,1)S(1)} fusion(bf16[1024,1024]{1,0:T(8,128)(2,1)S(1)} %copy-done.4, bf16[1024,1024]{1,0:T(8,128)(2,1)} %get-tuple-element.5, bf16[1024,1024]{1,0:T(8,128)(2,1)} %get-tuple-element.6, bf16[256,1024]{1,0:T(8,128)(2,1)S(1)} %get-tuple-element.26, bf16[256,1024]{1,0:T(8,128)(2,1)S(1)} %get-tuple-element.27), kind=kOutput, calls=%fused_computation.26 | convolution fusion | flops 2183659520 | bytes 8388608 | tf_op jit(solution)/shard_map/dot_general | solution.py:18
  57.9 53.8 %all_to_all.33 = bf16[2,8,1,32,1024]{4,3,2,0,1:T(8,128)(2,1)S(1)} all-to-all(bf16[2,8,1,32,1024]{4,3,2,0,1:T(8,128)(2,1)S(1)} %pad_maximum_fusion), channel_id=1, replica_groups=mesh['gx'=4,'gy'=2,'gz'=4] {'gy','gz'}, dimensions={1} | all-to-all | bytes 2097152 | tf_op jit(solution)/shard_map/all_to_all | solution.py:62
  111.6 3.2 %copy.44 = bf16[2,8,1,32,1024]{3,4,1,0,2:T(8,128)(2,1)} copy(bf16[2,8,1,32,1024]{4,3,2,0,1:T(8,128)(2,1)S(1)} %all_to_all.33) | data formatting | bytes 2097152 | tf_op jit(solution)/shard_map/all_to_all | solution.py:62
  114.8 3.9 %fusion.48 = (bf16[1,32,8,8,128]{1,2,4,3,0:T(8,128)(2,1)S(1)}, bf16[1,32,8,8,128]{1,2,4,3,0:T(8,128)(2,1)}) fusion(bf16[2,32,8,8,128]{1,2,4,3,0:T(8,128)(2,1)} %bitcast.75), kind=kLoop, calls=%fused_computation.63 | loop fusion | bytes 2097152 | tf_op jit(solution)/shard_map/slice | solution.py:29
  118.7 3.7 %copy.46 = bf16[1,32,8,8,128]{4,3,2,1,0:T(8,128)(2,1)S(1)} copy(bf16[1,32,8,8,128]{1,2,4,3,0:T(8,128)(2,1)} %get-tuple-element.8) | data formatting | bytes 1048576 | tf_op jit(solution)/shard_map/slice | solution.py:30
  122.6 2.0 copy.45
  124.6 1.0 copy.65
  125.5 1.9 fusion.45
  127.4 1.0 copy-done.3
  129.4 2.4 fusion.27
  132.0 1.2 copy.49
  133.2 3.8 %all-to-all-start.2 = ((bf16[2,1,32,8,8,128]{5,3,2,0,1,4:T(8,128)(2,1)}), bf16[2,1,32,8,8,128]{5,3,2,0,1,4:T(8,128)(2,1)S(1)}, u32[]{:S(2)}, u32[]{:S(2)}) async-start(bf16[2,1,32,8,8,128]{5,3,2,0,1,4:T(8,128)(2,1)} %copy.49), calls=%async_computation.2 | async-start | bytes 2097152 | tf_op jit(solution)/shard_map/all_to_all | solution.py:78
  137.0 77.9 %all-gather.7.cloned.1.call-done = bf16[1,2,1024,1024]{3,2,1,0:T(8,128)(2,1)} async-done(((bf16[1,2,256,1024]{3,2,1,0:T(8,128)(2,1)}), bf16[1,2,1024,1024]{3,2,1,0:T(8,128)(2,1)}) %all-gather.7.cloned.1.call-update) | async-done | bytes 4194320 | tf_op jit(solution)/shard_map/all_gather | solution.py:37
  214.9 3.2 %fusion.46 = bf16[1024,1024]{1,0:T(8,128)(2,1)} fusion(bf16[1,2,1024,1024]{3,2,1,0:T(8,128)(2,1)} %all-gather.7.cloned.1.call-done), kind=kLoop, calls=%fused_computation.61 | loop fusion | flops 1048576 | bytes 4194304 | tf_op jit(solution)/shard_map/neg | solution.py:12
  218.1 2.4 slice_bitcast_fusion
  220.8 1.3 copy-done.5
  222.1 0.6 copy-done.6
  222.7 19.6 %fusion.24 = bf16[256,2048]{1,0:T(8,128)(2,1)S(1)} fusion(bf16[1024,1024]{1,0:T(8,128)(2,1)} %get-tuple-element.14, bf16[1024,1024]{1,0:T(8,128)(2,1)S(1)} %copy-done.5, bf16[1024,1024]{1,0:T(8,128)(2,1)S(1)} %copy-done.6, bf16[256,1024]{1,0:T(8,128)(2,1)S(1)} %bitcast.88, bf16[256,1024]{1,0:T(8,128)(2,1)S(1)} %bitcast.89), kind=kOutput, calls=%fused_computation.24 | convolution fusion | flops 2183659520 | bytes 8388608 | tf_op jit(solution)/shard_map/dot_general | solution.py:32
  242.4 1.1 pad_maximum_fusion.2
  (31 shorter events, 2.1 us)
Async XLA Ops:
  6.5 13.6 %copy-start = (bf16[2,2,256,1024]{3,2,1,0:T(8,128)(2,1)S(1)}, bf16[2,2,256,1024]{3,2,1,0:T(8,128)(2,1)}, u32[]{:S(2)}) copy-start(bf16[2,2,256,1024]{3,2,1,0:T(8,128)(2,1)} %param.8) | copy-start | bytes 6291460
  6.5 5.3 %copy-start.7 = (bf16[2,1,1,1,256,1024]{5,4,3,2,1,0:T(8,128)(2,1)S(1)}, bf16[2,1,1,1,256,1024]{5,4,3,2,1,0:T(8,128)(2,1)}, u32[]{:S(2)}) copy-start(bf16[2,1,1,1,256,1024]{5,4,3,2,1,0:T(8,128)(2,1)} %param.5) | copy-start | bytes 3145732
  6.5 119.0 %all-gather.5.cloned.1.call-start = ((), (), s32[]{:S(2)}) async-start(), calls=%async_computation.3 | async-start | bytes 4718592 | tf_op jit(solution)/shard_map/all_gather | solution.py:75
  13.0 25.7 %all-to-all-start = ((bf16[2,1,8,32,1024]{4,3,1,0,2:T(8,128)(2,1)}), bf16[2,1,8,32,1024]{4,3,1,0,2:T(8,128)(2,1)S(1)}, u32[]{:S(2)}, u32[]{:S(2)}) async-start(bf16[2,1,8,32,1024]{4,3,1,0,2:T(8,128)(2,1)} %copy.38), calls=%async_computation | async-start | bytes 2097152 | tf_op jit(solution)/shard_map/all_to_all | solution.py:52
  18.1 196.7 %all-gather.7.cloned.1.call-start = ((), (), s32[]{:S(2)}) async-start(), calls=%async_computation.4 | async-start | bytes 5242880 | tf_op jit(solution)/shard_map/all_gather | solution.py:37
  51.3 1.9 copy-start.4
  125.5 2.8 %copy-start.3 = (bf16[1,2,1024,1024]{3,2,1,0:T(8,128)(2,1)S(1)}, bf16[1,2,1024,1024]{3,2,1,0:T(8,128)(2,1)}, u32[]{:S(2)}) copy-start(bf16[1,2,1024,1024]{3,2,1,0:T(8,128)(2,1)} %all-gather.5.cloned.1.call-done) | copy-start | bytes 12582916
  128.4 1.0 copy-start.8
  133.2 87.3 %all-to-all-start.2 = ((bf16[2,1,32,8,8,128]{5,3,2,0,1,4:T(8,128)(2,1)}), bf16[2,1,32,8,8,128]{5,3,2,0,1,4:T(8,128)(2,1)S(1)}, u32[]{:S(2)}, u32[]{:S(2)}) async-start(bf16[2,1,32,8,8,128]{5,3,2,0,1,4:T(8,128)(2,1)} %copy.49), calls=%async_computation.2 | async-start | bytes 2097152 | tf_op jit(solution)/shard_map/all_to_all | solution.py:78
  214.9 3.2 %copy-start.2 = (bf16[1,2,1024,1024]{3,2,1,0:T(8,128)(2,1)S(1)}, bf16[1,2,1024,1024]{3,2,1,0:T(8,128)(2,1)}, u32[]{:S(2)}) copy-start(bf16[1,2,1024,1024]{3,2,1,0:T(8,128)(2,1)} %all-gather.7.cloned.1.call-done) | copy-start | bytes 12582916
  220.5 1.6 copy-start.5
  220.5 2.2 copy-start.6
  222.7 20.8 %copy-start.1 = (bf16[2,2,256,1024]{3,2,1,0:T(8,128)(2,1)S(1)}, bf16[2,2,256,1024]{3,2,1,0:T(8,128)(2,1)}, u32[]{:S(2)}) copy-start(bf16[2,2,256,1024]{3,2,1,0:T(8,128)(2,1)} %param.8) | copy-start | bytes 6291460
Sparse Core Ops, SparseCore 0:
  11.9 99.0 all-gather.4
  112.5 102.2 all-gather.6
where the time goes:
time: 251 us; the launch traced here: 250 us
  waiting for transfers between devices  86.5 us (34%)
  blocking collectives  53.8 us (21%)
  local copies, waits for them, and re-layouts  45.1 us (18%)
  matrix products  26.6 us (11%)
  between operations  19.3 us (8%)
  other arithmetic  10.2 us (4%)
  starting transfers between devices  8.99 us (4%)
    all_gather x1, waiting for transfers between devices, third_contraction(): lax.all_gather(local_third, 'gz', axis=1, tiled=True)  77.9 us
    all_to_all x1, blocking collectives, body(): lax.all_to_all(middle.reshape(2, group_two, 1, rows_two, WIDTH), ('gy', '...  53.8 us
    dot_general x2, matrix products, make_accumulate(): jnp.dot(joined, complex_matrix(shard_rows), preferred_element_type=jnp.fl...  22 us
    slice x3, local copies, waits for them, and re-layouts, complex_product(): joined = jnp.concatenate([operand[0], operand[1]], axis=1)  9.42 us
    neg x3, other arithmetic, complex_matrix(): bottom_half = jnp.concatenate([-branch[1], branch[0]], axis=1)  8.94 us
    all_to_all x1, waiting for transfers between devices, body(): lax.all_to_all(stem.reshape(2, 1, group_one, rows_one, WIDTH), ('gx', 'gy...  8.57 us
    unnamed x22, local copies, waits for them, and re-layouts  6.38 us
    squeeze x3, local copies, waits for them, and re-layouts, complex_matrix(): top_half = jnp.concatenate([branch[0], branch[1]], axis=1)  6.04 us
  transfers between devices with their start and end apart: 4, of which 2 were waited for; matrix products, arithmetic and copies ran while one was open for 21% of the time, Pallas kernels for 0%

commit v1 on v0

--- a/solution.py
+++ b/solution.py
@@ -5,6 +5,18 @@
 
 WIDTH = 1024
 ROWS = 256
+
+
+def doubled_up(x, axis, dim):
+    ways, here, step = (lax.axis_size(axis), lax.axis_index(axis), x.shape[dim])
+    line, have = (x, 1)
+    while have < ways:
+        line = jnp.concatenate(
+            [line, lax.ppermute(line, axis, [(d, (d - have) % ways) for d in range(ways)])],
+            axis=dim,
+        )
+        have = 2 * have
+    return jnp.roll(line, here * step, axis=dim)
 
 
 def complex_matrix(branch):
@@ -34,7 +46,7 @@
 
 def third_contraction(operand, branch_three, slice_values):
     local_third = lax.dynamic_index_in_dim(branch_three, slice_values[2], 0, keepdims=False)
-    summed = make_accumulate(operand, lax.all_gather(local_third, "gz", axis=1, tiled=True))
+    summed = make_accumulate(operand, doubled_up(local_third, "gz", 1))
     return split_result(summed).astype(jnp.bfloat16)
 
 

time: 251 us -> 294 us (1.17)
  waiting for transfers between devices: 86.5 us -> 155 us
  blocking collectives: 53.8 us -> 32.5 us
  matrix products: 26.6 us -> 7.18 us
  local copies, waits for them, and re-layouts: 45.1 us -> 58 us
  starting transfers between devices: 8.99 us -> 13.3 us
    ppermute x0 -> x2, waiting for transfers between devices: none -> 122 us  [doubled_up(): lax.ppermute(line, axis, [(d, (d - have) % ways) for d in range(ways)])]
    all_gather x1 -> x0, waiting for transfers between devices: 77.9 us -> none  [third_contraction(): lax.all_gather(local_third, 'gz', axis=1, tiled=True)]
    all_to_all x1, waiting for transfers between devices: 0.01 us -> 22.1 us  [body(): lax.all_to_all(second.reshape(2, 1, rows_two, group_two, group_two, part_...]
    all_to_all x1, blocking collectives: 53.8 us -> 32.5 us  [body(): lax.all_to_all(middle.reshape(2, group_two, 1, rows_two, WIDTH), ('gy', '...]
    dot_general x2, matrix products: 22 us -> 4.79 us  [make_accumulate(): jnp.dot(joined, complex_matrix(shard_rows), preferred_element_type=jnp.fl...]
    unnamed x22 -> x27, local copies, waits for them, and re-layouts: 6.38 us -> 13.2 us
    ppermute x0 -> x2, starting transfers between devices: none -> 5.05 us  [doubled_up(): lax.ppermute(line, axis, [(d, (d - have) % ways) for d in range(ways)])]
    squeeze x3, local copies, waits for them, and re-layouts: 6.04 us -> 9.25 us  [complex_matrix(): top_half = jnp.concatenate([branch[0], branch[1]], axis=1)]
  transfers between devices with their start and end apart: 4 -> 5, of which waited for: 2 -> 4; matrix products, arithmetic and copies ran while one was open for 21% -> 19% of each run, Pallas kernels for 0% -> 0%
where the time goes in v1:
time: 294 us
  waiting for transfers between devices  155 us (53%)
  local copies, waits for them, and re-layouts  58 us (20%)
  blocking collectives  32.5 us (11%)
  between operations  19.2 us (7%)
  starting transfers between devices  13.3 us (5%)
  other arithmetic  8.64 us (3%)
  matrix products  7.18 us (2%)
    ppermute x2, waiting for transfers between devices, doubled_up(): lax.ppermute(line, axis, [(d, (d - have) % ways) for d in range(ways)])  122 us
    all_to_all x1, blocking collectives, body(): lax.all_to_all(middle.reshape(2, group_two, 1, rows_two, WIDTH), ('gy', '...  32.5 us
    all_to_all x1, waiting for transfers between devices, body(): lax.all_to_all(second.reshape(2, 1, rows_two, group_two, group_two, part_...  22.1 us
    unnamed x27, local copies, waits for them, and re-layouts  13.2 us
    slice x3, local copies, waits for them, and re-layouts, complex_product(): joined = jnp.concatenate([operand[0], operand[1]], axis=1)  11.6 us
    all_to_all x1, waiting for transfers between devices, body(): lax.all_to_all(stem.reshape(2, 1, group_one, rows_one, WIDTH), ('gx', 'gy...  10.1 us
    squeeze x3, local copies, waits for them, and re-layouts, complex_matrix(): top_half = jnp.concatenate([branch[0], branch[1]], axis=1)  9.25 us
    slice x3, local copies, waits for them, and re-layouts, make_accumulate(): real_part = operand[0]  5.98 us
  transfers between devices with their start and end apart: 5, of which 4 were waited for; matrix products, arithmetic and copies ran while one was open for 19% of the time, Pallas kernels for 0%

profile of v1, /device:TPU:0, one launch (start us, length us, event | category | flops | bytes accessed | tf_op | source)
XLA Modules:
  0.0 293.5 jit_solution(11697151875386247697)
XLA Ops:
  6.5 1.4 fusion.52
  9.9 2.5 constant_dynamic-update-slice_fusion.5
  12.3 5.0 %collective-permute-start = (bf16[2,256,1024]{2,1,0:T(8,128)(2,1)S(1)}, bf16[2,256,1024]{2,1,0:T(8,128)(2,1)S(1)}, u32[]{:S(2)}, u32[]{:S(2)}) collective-permute-start(bf16[2,256,1024]{2,1,0:T(8,128)(2,1)S(1)} %get-tuple-element.10), channel_id=1, source_target_pairs={{0,3},{1,0},{2,1},{3,2},{4,7},{5,4},{6,5},{7,6},{8,11},{9,8},{10,9... | collective-permute-start | bytes 3145736 | tf_op jit(solution)/shard_map/ppermute | solution.py:15
  20.2 34.1 %collective-permute-done = bf16[2,256,1024]{2,1,0:T(8,128)(2,1)S(1)} collective-permute-done((bf16[2,256,1024]{2,1,0:T(8,128)(2,1)S(1)}, bf16[2,256,1024]{2,1,0:T(8,128)(2,1)S(1)}, u32[]{:S(2)}, u32[]{:S(2)}) %collective-permute-start) | collective-permute-done | bytes 1048608 | tf_op jit(solution)/shard_map/ppermute | solution.py:15
  54.2 1.5 pad_maximum_fusion
  55.8 1.1 copy.38
  56.8 4.7 %all-to-all-start = ((bf16[2,1,8,32,1024]{4,3,1,0,2:T(8,128)(2,1)}), bf16[2,1,8,32,1024]{4,3,1,0,2:T(8,128)(2,1)S(1)}, u32[]{:S(2)}, u32[]{:S(2)}) async-start(bf16[2,1,8,32,1024]{4,3,1,0,2:T(8,128)(2,1)} %copy.38), calls=%async_computation | async-start | bytes 2097152 | tf_op jit(solution)/shard_map/all_to_all | solution.py:64
  63.3 3.1 %dynamic-slice_bitcast_fusion.3 = bf16[1024,1024]{1,0:T(8,128)(2,1)} fusion(bf16[2,2,1024,1024]{3,2,1,0:T(8,128)(2,1)} %param.6, s32[]{:T(128)S(6)} %select_n.25), kind=kLoop, calls=%fused_computation.32 | loop fusion | bytes 4194308 | tf_op jit(solution)/shard_map/squeeze | solution.py:23
  66.4 10.1 %all-to-all-done = bf16[2,1,8,32,1024]{4,3,1,0,2:T(8,128)(2,1)S(1)} async-done(((bf16[2,1,8,32,1024]{4,3,1,0,2:T(8,128)(2,1)}), bf16[2,1,8,32,1024]{4,3,1,0,2:T(8,128)(2,1)S(1)}, u32[]{:S(2)}, u32[]{:S(2)}) %all-to-all-start) | async-done | bytes 1048608 | tf_op jit(solution)/shard_map/all_to_all | solution.py:64
  76.5 3.1 %copy.39 = bf16[2,1,8,32,1024]{3,4,2,0,1:T(8,128)(2,1)} copy(bf16[2,1,8,32,1024]{4,3,1,0,2:T(8,128)(2,1)S(1)} %all-to-all-done) | data formatting | bytes 2097152 | tf_op jit(solution)/shard_map/all_to_all | solution.py:64
  79.6 4.7 %fusion.49 = (bf16[1,32,8,8,128]{1,2,4,3,0:T(8,128)(2,1)}, bf16[1,32,8,8,128]{1,2,4,3,0:T(8,128)(2,1)}) fusion(bf16[2,32,8,8,128]{1,2,4,3,0:T(8,128)(2,1)} %bitcast.76), kind=kLoop, calls=%fused_computation.71 | loop fusion | bytes 2097152 | tf_op jit(solution)/shard_map/slice | solution.py:29
  84.3 3.5 %copy.41 = bf16[1,32,8,8,128]{4,3,2,1,0:T(8,128)(2,1)S(1)} copy(bf16[1,32,8,8,128]{1,2,4,3,0:T(8,128)(2,1)} %get-tuple-element.14) | data formatting | bytes 1048576 | tf_op jit(solution)/shard_map/slice | solution.py:29
  87.8 3.5 %copy.40 = bf16[1,32,8,8,128]{4,3,2,1,0:T(8,128)(2,1)S(1)} copy(bf16[1,32,8,8,128]{1,2,4,3,0:T(8,128)(2,1)} %get-tuple-element.13) | data formatting | bytes 1048576 | tf_op jit(solution)/shard_map/slice | solution.py:29
  92.5 88.4 %collective-permute-done.1 = bf16[2,512,1024]{2,1,0:T(8,128)(2,1)} collective-permute-done((bf16[2,512,1024]{2,1,0:T(8,128)(2,1)}, bf16[2,512,1024]{2,1,0:T(8,128)(2,1)}, u32[]{:S(2)}, u32[]{:S(2)}) %collective-permute-start.1) | collective-permute-done | bytes 2097184 | tf_op jit(solution)/shard_map/ppermute | solution.py:15
  180.9 3.1 %constant_dynamic-update-slice_fusion.3 = bf16[2,2048,1024]{2,1,0:T(8,128)(2,1)} fusion(bf16[2,2048,1024]{2,1,0:T(8,128)(2,1)} %constant_dynamic-update-slice_fusion.4, bf16[2,512,1024]{2,1,0:T(8,128)(2,1)} %collective-permute-done.1), kind=kLoop, calls=%fused_computation.60 | loop fusion | bytes 4194304
  186.1 3.2 %constant_dynamic-update-slice_fusion = bf16[2,2048,1024]{2,1,0:T(8,128)(2,1)} fusion(bf16[2,2048,1024]{2,1,0:T(8,128)(2,1)} %constant_dynamic-update-slice_fusion.1, bf16[2,512,1024]{2,1,0:T(8,128)(2,1)} %collective-permute-done.1), kind=kLoop, calls=%fused_computation.57 | loop fusion | bytes 4194304 | tf_op jit(solution)/shard_map/jit(_roll_dynamic)/concatenate | solution.py:19
  189.3 5.7 %fusion.46 = (bf16[1024,1024]{1,0:T(8,128)(2,1)S(1)}, bf16[1024,1024]{1,0:T(8,128)(2,1)S(1)}, bf16[1024,1024]{1,0:T(8,128)(2,1)}, bf16[1024,1024]{1,0:T(8,128)(2,1)}) fusion(bf16[2,2,1024,1024]{3,2,1,0:T(8,128)(2,1)} %param.6, s32[]{:T(128)S(6)} %select_n.25, s32[]{:T(128)S(6)} %add.27, bf16[2,2048,1024]{2,1,0:T(8,128)(2,1)} %constant_dynamic-update-slice_fusion, ...), kind=kLoop, calls=%fused_computation.68 | loop fusion | flops 6291456 | bytes 12582924 | tf_op jit(solution)/shard_map/neg | solution.py:24
  195.0 2.4 fusion.30
  197.6 32.5 %all_to_all.33 = bf16[2,8,1,32,1024]{4,3,2,0,1:T(8,128)(2,1)S(1)} all-to-all(bf16[2,8,1,32,1024]{4,3,2,0,1:T(8,128)(2,1)S(1)} %pad_maximum_fusion.1), channel_id=1, replica_groups=mesh['gx'=4,'gy'=2,'gz'=4] {'gy','gz'}, dimensions={1} | all-to-all | bytes 2097152 | tf_op jit(solution)/shard_map/all_to_all | solution.py:74
  230.0 3.1 %copy.44 = bf16[2,8,1,32,1024]{3,4,1,0,2:T(8,128)(2,1)} copy(bf16[2,8,1,32,1024]{4,3,2,0,1:T(8,128)(2,1)S(1)} %all_to_all.33) | data formatting | bytes 2097152 | tf_op jit(solution)/shard_map/all_to_all | solution.py:74
  233.2 3.9 %fusion.48 = (bf16[1,32,8,8,128]{1,2,4,3,0:T(8,128)(2,1)S(1)}, bf16[1,32,8,8,128]{1,2,4,3,0:T(8,128)(2,1)}) fusion(bf16[2,32,8,8,128]{1,2,4,3,0:T(8,128)(2,1)} %bitcast.77), kind=kLoop, calls=%fused_computation.70 | loop fusion | bytes 2097152 | tf_op jit(solution)/shard_map/slice | solution.py:41
  237.1 3.5 %copy.46 = bf16[1,32,8,8,128]{4,3,2,1,0:T(8,128)(2,1)S(1)} copy(bf16[1,32,8,8,128]{1,2,4,3,0:T(8,128)(2,1)} %get-tuple-element.12) | data formatting | bytes 1048576 | tf_op jit(solution)/shard_map/slice | solution.py:42
  241.5 2.0 copy.45
  243.6 2.8 slice_bitcast_fusion
  248.1 2.4 fusion.27
  250.7 1.2 copy.49
  251.9 3.6 %all-to-all-start.2 = ((bf16[2,1,32,8,8,128]{5,3,2,0,1,4:T(8,128)(2,1)}), bf16[2,1,32,8,8,128]{5,3,2,0,1,4:T(8,128)(2,1)S(1)}, u32[]{:S(2)}, u32[]{:S(2)}) async-start(bf16[2,1,32,8,8,128]{5,3,2,0,1,4:T(8,128)(2,1)} %copy.49), calls=%async_computation.2 | async-start | bytes 2097152 | tf_op jit(solution)/shard_map/all_to_all | solution.py:90
  255.5 3.3 %dynamic-slice_bitcast_fusion.1 = bf16[1024,1024]{1,0:T(8,128)(2,1)} fusion(bf16[2,2048,1024]{2,1,0:T(8,128)(2,1)} %constant_dynamic-update-slice_fusion, s32[]{:T(128)S(6)} %select_n.29), kind=kLoop, calls=%fused_computation.28 | loop fusion | bytes 4194308 | tf_op jit(solution)/shard_map/squeeze | solution.py:23
  258.8 22.1 %all-to-all-done.2 = bf16[2,1,32,8,8,128]{5,3,2,0,1,4:T(8,128)(2,1)S(1)} async-done(((bf16[2,1,32,8,8,128]{5,3,2,0,1,4:T(8,128)(2,1)}), bf16[2,1,32,8,8,128]{5,3,2,0,1,4:T(8,128)(2,1)S(1)}, u32[]{:S(2)}, u32[]{:S(2)}) %all-to-all-start.2) | async-done | bytes 1048608 | tf_op jit(solution)/shard_map/all_to_all | solution.py:90
  281.2 1.3 copy-done.4
  283.2 2.4 fusion.24
  285.6 1.1 pad_maximum_fusion.3
  (37 shorter events, 8.2 us)
Async XLA Ops:
  6.5 12.8 %copy-start = (bf16[2,2,128,1024]{3,2,1,0:T(8,128)(2,1)S(1)}, bf16[2,2,128,1024]{3,2,1,0:T(8,128)(2,1)}, u32[]{:S(2)}) copy-start(bf16[2,2,128,1024]{3,2,1,0:T(8,128)(2,1)} %param.7) | copy-start | bytes 3145732
  6.5 237.0 %all-gather.3.cloned.1.call-start = ((), (), s32[]{:S(2)}) async-start(), calls=%async_computation.3 | async-start | bytes 4718592 | tf_op jit(solution)/shard_map/all_gather | solution.py:87
  12.3 41.9 %collective-permute-start = (bf16[2,256,1024]{2,1,0:T(8,128)(2,1)S(1)}, bf16[2,256,1024]{2,1,0:T(8,128)(2,1)S(1)}, u32[]{:S(2)}, u32[]{:S(2)}) collective-permute-start(bf16[2,256,1024]{2,1,0:T(8,128)(2,1)S(1)} %get-tuple-element.10), channel_id=1, source_target_pairs={{0,3},{1,0},{2,1},{3,2},{4,7},{5,4},{6,5},{7,6},{8,11},{9,8},{10,9... | collective-permute-start | bytes 3145736 | tf_op jit(solution)/shard_map/ppermute | solution.py:15
  20.2 35.6 %copy-start.7 = (bf16[2,1,1,1,256,1024]{5,4,3,2,1,0:T(8,128)(2,1)S(1)}, bf16[2,1,1,1,256,1024]{5,4,3,2,1,0:T(8,128)(2,1)}, u32[]{:S(2)}) copy-start(bf16[2,1,1,1,256,1024]{5,4,3,2,1,0:T(8,128)(2,1)} %param.5) | copy-start | bytes 3145732
  55.8 125.2 %collective-permute-start.1 = (bf16[2,512,1024]{2,1,0:T(8,128)(2,1)}, bf16[2,512,1024]{2,1,0:T(8,128)(2,1)}, u32[]{:S(2)}, u32[]{:S(2)}) collective-permute-start(bf16[2,512,1024]{2,1,0:T(8,128)(2,1)} %pad_maximum_fusion), channel_id=1, source_target_pairs={{0,2},{1,3},{2,0},{3,1},{4,6},{5,7},{6,4},{7,5},{8,10},{9,11},{10,... | collective-permute-start | bytes 6291464 | tf_op jit(solution)/shard_map/ppermute | solution.py:15
  56.8 19.7 %all-to-all-start = ((bf16[2,1,8,32,1024]{4,3,1,0,2:T(8,128)(2,1)}), bf16[2,1,8,32,1024]{4,3,1,0,2:T(8,128)(2,1)S(1)}, u32[]{:S(2)}, u32[]{:S(2)}) async-start(bf16[2,1,8,32,1024]{4,3,1,0,2:T(8,128)(2,1)} %copy.38), calls=%async_computation | async-start | bytes 2097152 | tf_op jit(solution)/shard_map/all_to_all | solution.py:64
  189.3 5.7 %copy-start.5 = (bf16[1024,1024]{1,0:T(8,128)(2,1)S(1)}, bf16[1024,1024]{1,0:T(8,128)(2,1)}, u32[]{:S(2)}) copy-start(bf16[1024,1024]{1,0:T(8,128)(2,1)} %dynamic-slice_bitcast_fusion.3) | copy-start | bytes 6291460
  243.6 3.5 %copy-start.2 = (bf16[1,2,1024,1024]{3,2,1,0:T(8,128)(2,1)S(1)}, bf16[1,2,1024,1024]{3,2,1,0:T(8,128)(2,1)}, u32[]{:S(2)}) copy-start(bf16[1,2,1024,1024]{3,2,1,0:T(8,128)(2,1)} %all-gather.3.cloned.1.call-done) | copy-start | bytes 12582916
  247.0 1.0 copy-start.8
  251.9 29.0 %all-to-all-start.2 = ((bf16[2,1,32,8,8,128]{5,3,2,0,1,4:T(8,128)(2,1)}), bf16[2,1,32,8,8,128]{5,3,2,0,1,4:T(8,128)(2,1)S(1)}, u32[]{:S(2)}, u32[]{:S(2)}) async-start(bf16[2,1,32,8,8,128]{5,3,2,0,1,4:T(8,128)(2,1)} %copy.49), calls=%async_computation.2 | async-start | bytes 2097152 | tf_op jit(solution)/shard_map/all_to_all | solution.py:90
  255.5 25.7 %copy-start.3 = (bf16[1024,1024]{1,0:T(8,128)(2,1)S(1)}, bf16[1024,1024]{1,0:T(8,128)(2,1)}, u32[]{:S(2)}) copy-start(bf16[1024,1024]{1,0:T(8,128)(2,1)} %get-tuple-element.28) | copy-start | bytes 6291460
  280.9 1.6 copy-start.4
  280.9 2.2 copy-start.6
  283.1 3.5 %copy-start.1 = (bf16[2,2,128,1024]{3,2,1,0:T(8,128)(2,1)S(1)}, bf16[2,2,128,1024]{3,2,1,0:T(8,128)(2,1)}, u32[]{:S(2)}) copy-start(bf16[2,2,128,1024]{3,2,1,0:T(8,128)(2,1)} %param.7) | copy-start | bytes 3145732
Sparse Core Ops, SparseCore 0:
  20.3 144.4 all-gather.2
